TPU v7x, 32 devices: a whole 2x2x4 slice. The times are simulated.
32 devices in a mesh: dp: 16 (over z, y, core), ctx: 2 (over x).
Axes of the slice: x: 2, y: 2, z: 4, core: 2. Of those that a mesh axis runs over, the one named last changes fastest.
Arguments:
- frames: bfloat16 [16, 1024, 1280], P('dp', 'ctx'), may hold values from -6 to 6
- conv_taps: float32 [31, 1280], replicated, may hold values from -1 to 1
- conv_gain: float32 [1280], replicated, may hold values from 0.1 to 1.9
- w_kv: bfloat16 [1280, 2560], P('dp'), may hold values from -0.15625 to 0.15625
- queries: bfloat16 [16, 32, 1280], P('dp', 'ctx'), may hold values from -6 to 6
- out_grad: bfloat16 [16, 32, 1280], P('dp', 'ctx'), may hold values from -6 to 6
- frame_len: int32 [16], P('dp'), may hold values from 256 to 1024
- token_len: int32 [16], P('dp'), may hold values from 8 to 32
Outputs:
- frames_grad: bfloat16 [16, 1024, 1280], P('dp', 'ctx')
- taps_grad: float32 [31, 1280], replicated
- gain_grad: float32 [1280], replicated
- w_kv_grad: float32 [1280, 2560], P('dp')
- queries_grad: bfloat16 [16, 32, 1280], P('dp', 'ctx')
Inputs may be any that keep to these rules, and one draw needn't show every extreme that they name: frames at positions of frame_len[b] or beyond are padding of utterance b. Tokens at positions of token_len[b] or beyond are padding of utterance b.
All inputs are finite; a program needn't handle non-finite values.
Results may differ from a plain program's by a relative error of at most 0.012.
Values may be sent and summed in bfloat16 or wider, within the bound.
A program may use at most 128 MiB of HBM per device.

v0:
```python
import jax
import jax.numpy as jnp
from jax import lax
from jax.sharding import PartitionSpec as P

HEADS = 20


def padded_2(block, sides, width):
    for axis, dim in sides:
        count = lax.axis_size(axis)
        forward = [(i, i + 1) for i in range(count - 1)]
        backward = [(target, source) for source, target in forward]
        low = lax.ppermute(
            lax.slice_in_dim(block, block.shape[dim] - width, None, axis=dim), axis, forward
        )
        high = lax.ppermute(lax.slice_in_dim(block, 0, width, axis=dim), axis, backward)
        block = jnp.concatenate([low, block, high], axis=dim)
    return block


def shifted(value, axis, steps):
    count = lax.axis_size(axis)
    pairs = [(source, (source + steps) % count) for source in range(count)]
    return lax.ppermute(value, axis, pairs)


def conv_time(padded, conv_taps, length):
    total = jnp.zeros((length, padded.shape[1]), jnp.float32)
    for tap_idx in range(conv_taps.shape[0]):
        total = total + conv_taps[tap_idx] * padded[tap_idx : tap_idx + length].astype(jnp.float32)
    return total


def silu_slope(gated):
    sigma = jax.nn.sigmoid(gated)
    return sigma * (1.0 + gated * (1.0 - sigma))


def forward_part(query_block, key_block, value_block, live_mask, head_count):
    row_count = query_block.shape[0]
    frame_count = key_block.shape[0]
    q_heads = query_block.reshape(row_count, head_count, -1)
    k_heads = key_block.reshape(frame_count, head_count, -1)
    v_heads = value_block.reshape(frame_count, head_count, -1)
    scale = q_heads.shape[2] ** (-0.5)
    exp_scores = (
        jnp.exp(
            jnp.einsum("thd,fhd->htf", q_heads, k_heads, preferred_element_type=jnp.float32) * scale
        )
        * live_mask
    )
    totals = jnp.sum(exp_scores, axis=2).T
    weighted = jnp.einsum(
        "htf,fhd->thd", exp_scores.astype(jnp.bfloat16), v_heads, preferred_element_type=jnp.float32
    )
    return (weighted.reshape(row_count, -1), totals)


def backward_part(
    query_block, grad_block, totals, delta_rows, key_block, value_block, live_mask, head_count
):
    row_count = query_block.shape[0]
    frame_count = key_block.shape[0]
    q_heads = query_block.reshape(row_count, head_count, -1)
    g_heads = grad_block.reshape(row_count, head_count, -1)
    k_heads = key_block.reshape(frame_count, head_count, -1)
    v_heads = value_block.reshape(frame_count, head_count, -1)
    scale = q_heads.shape[2] ** (-0.5)
    exp_scores = (
        jnp.exp(
            jnp.einsum("thd,fhd->htf", q_heads, k_heads, preferred_element_type=jnp.float32) * scale
        )
        * live_mask
    )
    attn_prob = exp_scores / totals.T[:, :, None]
    d_prob = jnp.einsum("thd,fhd->htf", g_heads, v_heads, preferred_element_type=jnp.float32)
    d_score = (attn_prob * (d_prob - delta_rows.T[:, :, None])).astype(jnp.bfloat16)
    query_part = jnp.einsum(
        "htf,fhd->thd", d_score, k_heads, preferred_element_type=jnp.float32
    ).reshape(row_count, -1)
    key_part = jnp.einsum(
        "htf,thd->fhd", d_score, q_heads, preferred_element_type=jnp.float32
    ).reshape(frame_count, -1)
    value_part = jnp.einsum(
        "htf,thd->fhd", attn_prob.astype(jnp.bfloat16), g_heads, preferred_element_type=jnp.float32
    ).reshape(frame_count, -1)
    return (query_part, key_part, value_part)


def row_delta(weighted, totals, grad_block):
    row_count = weighted.shape[0]
    head_count = totals.shape[1]
    head_dim = weighted.shape[1] // head_count
    attended = weighted / jnp.repeat(totals, head_dim, axis=1)
    return jnp.sum(
        (grad_block.astype(jnp.float32) * attended).reshape(row_count, head_count, head_dim), axis=2
    )


def per_device(frames, conv_taps, conv_gain, w_kv, queries, out_grad, frame_len, token_len):
    cycle_size = lax.axis_size("ctx")
    cycle_pos = lax.axis_index("ctx")
    length = frames.shape[1]
    model_width = frames.shape[2]
    tokens = queries.shape[1]
    tap_count = conv_taps.shape[0]
    rim_width = tap_count // 2
    scale = (model_width // HEADS) ** (-0.5)
    padded = padded_2(frames, (("ctx", 1),), rim_width)[0]
    conv_out = conv_time(padded, conv_taps, length)
    gated = conv_gain * conv_out
    encoded = (frames[0].astype(jnp.float32) + jax.nn.silu(gated)).astype(jnp.bfloat16)
    w_full = lax.all_gather(w_kv, "dp", axis=0, tiled=True)
    key_values = jnp.dot(encoded, w_full, preferred_element_type=jnp.float32).astype(jnp.bfloat16)
    key_block = key_values[:, :model_width]
    value_block = key_values[:, model_width:]
    frame_pos = cycle_pos * length + jnp.arange(length)
    live_mask = (frame_pos < frame_len[0]).astype(jnp.float32)
    token_pos = cycle_pos * tokens + jnp.arange(tokens)
    grad_block = out_grad[0] * (token_pos < token_len[0]).astype(jnp.bfloat16)[:, None]
    query_block = queries[0]

    def forward_tile(visitor, keys_part, values_part, head_count):
        return forward_part(visitor, keys_part, values_part, live_mask, head_count)

    def backward_tile(
        visitor, visit_grad, visit_totals, visit_delta, keys_part, values_part, head_count
    ):
        return backward_part(
            visitor,
            visit_grad,
            visit_totals,
            visit_delta,
            keys_part,
            values_part,
            live_mask,
            head_count,
        )

    def forward_turn(turn_idx, carried):
        visitor, weighted, totals = carried
        part_sum, part_total = forward_tile(visitor, key_block, value_block, HEADS)
        visitor = shifted(visitor, "ctx", 1)
        weighted, totals = shifted((weighted + part_sum, totals + part_total), "ctx", 1)
        return (visitor, weighted, totals)

    first_state = (
        query_block,
        jnp.zeros((tokens, model_width), jnp.float32),
        jnp.zeros((tokens, HEADS), jnp.float32),
    )
    first_out = lax.fori_loop(0, cycle_size, forward_turn, first_state)
    totals = first_out[2]
    delta_rows = row_delta(first_out[1], totals, grad_block)

    def backward_turn(turn_idx, carried):
        visitor, visit_grad, visit_totals, visit_delta, query_acc, key_acc, value_acc = carried
        part_query, part_key, part_value = backward_tile(
            visitor, visit_grad, visit_totals, visit_delta, key_block, value_block, HEADS
        )
        visitor, visit_grad = shifted((visitor, visit_grad), "ctx", 1)
        visit_totals, visit_delta, query_acc = shifted(
            (visit_totals, visit_delta, query_acc + part_query), "ctx", 1
        )
        return (
            visitor,
            visit_grad,
            visit_totals,
            visit_delta,
            query_acc,
            key_acc + part_key,
            value_acc + part_value,
        )

    second_state = (
        query_block,
        grad_block,
        totals,
        delta_rows,
        jnp.zeros((tokens, model_width), jnp.float32),
        jnp.zeros((length, model_width), jnp.float32),
        jnp.zeros((length, model_width), jnp.float32),
    )
    second_out = lax.fori_loop(0, cycle_size, backward_turn, second_state)
    query_acc = second_out[4]
    key_acc = second_out[5]
    value_acc = second_out[6]
    queries_grad = (query_acc * scale).astype(jnp.bfloat16)[None]
    kv_grad = jnp.concatenate([key_acc * scale, value_acc], 1).astype(jnp.bfloat16)
    enc_grad = lax.dot_general(
        kv_grad, w_full, (((1,), (1,)), ((), ())), preferred_element_type=jnp.float32
    )
    gated_grad = enc_grad * silu_slope(gated)
    gain_term = jnp.sum(gated_grad * conv_out, axis=0)
    conv_grad = gated_grad * conv_gain
    tap_terms = jnp.stack(
        [
            jnp.sum(conv_grad * padded[tap_idx : tap_idx + length].astype(jnp.float32), axis=0)
            for tap_idx in range(tap_count)
        ]
    )
    padded_grad = padded_2(conv_grad[None], (("ctx", 1),), rim_width)[0]
    back_conv = jnp.zeros((length, model_width), jnp.float32)
    for tap_idx in range(tap_count):
        offset = 2 * rim_width - tap_idx
        back_conv = back_conv + conv_taps[tap_idx] * padded_grad[offset : offset + length]
    frames_grad = (enc_grad + back_conv).astype(jnp.bfloat16)[None]
    taps_grad, gain_grad = lax.psum((tap_terms, gain_term), ("dp", "ctx"))
    data_part = lax.psum_scatter(
        lax.dot_general(
            encoded, kv_grad, (((0,), (0,)), ((), ())), preferred_element_type=jnp.float32
        ),
        "dp",
        scatter_dimension=0,
        tiled=True,
    )
    w_kv_grad = lax.psum(data_part, "ctx")
    return (frames_grad, taps_grad, gain_grad, w_kv_grad, queries_grad)


def solution(mesh):
    placed = (
        P("dp", "ctx", None),
        P(),
        P(),
        P("dp", None),
        P("dp", "ctx", None),
        P("dp", "ctx", None),
        P("dp"),
        P("dp"),
    )
    return jax.shard_map(
        per_device,
        mesh=mesh,
        in_specs=placed,
        out_specs=(P("dp", "ctx", None), P(), P(), P("dp", None), P("dp", "ctx", None)),
        check_vma=False,
    )
```

profile of v0, /device:TPU:0, one launch (start us, length us, event | category | flops | bytes accessed | tf_op | source)
XLA Modules:
  0.0 496.1 jit_solution(5663490250576671858)
XLA Ops:
  7.2 1.5 copy.116
  9.6 4.8 collective-permute-start.8
  18.0 1.8 slice_reduce_fusion.30
  19.9 1.5 constant_dynamic-update-slice_fusion.1
  22.3 12.4 %fusion.82 = (bf16[512,1280]{1,0:T(8,128)(2,1)}, f32[512,1280]{1,0:T(8,128)}) fusion(bf16[1,512,1280]{2,1,0:T(8,128)(2,1)S(1)} %copy-done.4, f32[1280]{0:T(1024)S(1)} %copy-done.75, bf16[1,527,1280]{2,1,0:T(8,128)(2,1)S(1)} %constant_dynamic-update-slice_fusion, f32[1280]{0:T(1024)S(1)} %get-tuple-element.290, f32[1280]{0:T(1024)S(1)} %get-tuple-element.291, ...), kind=kLoop, calls=%fused_computation.196 | loop fusion | flops 104202240 | bytes 25105920 | tf_op jit(solution)/shard_map/convert_element_type | solution.py:113
  35.0 41.4 %all-gather.2.cloned.1.call-done = bf16[1280,2560]{1,0:T(8,128)(2,1)} async-done(((bf16[80,2560]{1,0:T(8,128)(2,1)}), bf16[1280,2560]{1,0:T(8,128)(2,1)}) %all-gather.2.cloned.1.call-update) | async-done | bytes 6553616 | tf_op jit(solution)/shard_map/all_gather | solution.py:114
  76.4 6.8 %convolution_convert_fusion = bf16[512,2560]{1,0:T(8,128)(2,1)S(1)} fusion(bf16[512,1280]{1,0:T(8,128)(2,1)} %get-tuple-element.335, bf16[1280,2560]{1,0:T(8,128)(2,1)} %all-gather.2.cloned.1.call-done), kind=kOutput, calls=%fused_computation.72 | convolution fusion | flops 3356753920 | bytes 10485760 | tf_op jit(solution)/shard_map/dot_general | solution.py:115
  83.3 1.7 fusion.242
  85.0 1.6 copy.43
  86.6 2.4 copy.42
  89.6 19.6 %while.38 = (s32[]{:T(128)}, bf16[16,1280]{1,0:T(8,128)(2,1)S(1)}, f32[16,1280]{1,0:T(8,128)S(1)}, f32[16,20]{0,1:T(8,128)}, bf16[512,1280]{0,1:T(8,128)(2,1)}, ...) while((s32[]{:T(128)}, bf16[16,1280]{1,0:T(8,128)(2,1)S(1)}, ...), condition=%wide.region_2.3_spmd.clone, body=%wide.region_0.2_spmd.clone.sunk | while | flops 42620416 | bytes 4643037 | solution.py:153
  89.7 1.5 collective-permute-start
  92.0 1.7 fusion.280
  95.7 1.5 collective-permute-start.2
  97.1 2.3 collective-permute-done.2
  99.5 1.5 collective-permute-start
  101.8 1.7 fusion.280
  105.5 1.5 collective-permute-start.2
  106.9 2.3 collective-permute-done.2
  112.5 56.3 %while.39 = (s32[]{:T(128)}, bf16[16,1280]{1,0:T(8,128)(2,1)}, bf16[16,1280]{1,0:T(8,128)(2,1)}, f32[16,20]{0,1:T(8,128)}, f32[16,20]{0,1:T(8,128)}, /*index=5*/...) while((s32[]{:T(128)}, bf16[16,1280]{1,0:T(8,128)(2,1)}, ...), condition=%wide.region_5.6_spmd.clone, body=%wide.region_4.5_spmd.clone.sunk | while | flops 108647936 | bytes 37869488 | solution.py:185
  113.8 1.5 collective-permute-start.5
  117.9 1.5 collective-permute-start.3
  121.6 1.7 fusion.292
  126.7 1.5 collective-permute-start.7
  128.3 3.1 fusion.294
  131.4 2.1 fusion.295
  133.5 6.1 %bitcast_add_fusion.6 = (f32[512,1280]{0,1:T(8,128)}, f32[512,1280]{0,1:T(8,128)}) fusion(f32[20,512,64]{1,2,0:T(8,128)} %fusion.294, f32[512,1280]{0,1:T(8,128)} %get-tuple-element.528, pred[]{:T(512)S(6)} %compare.3, f32[20,512,64]{1,2,0:T(8,128)} %fusion.295, f32[512,1280]{0,1:T(8,128)} %get-tuple-element.527), kind=kLoop, calls=%fused_computation.11.clone.1 | loop fusion | flops 2621440 | bytes 15728641 | tf_op jit(solution)/shard_map/while/body/eval_jaxpr/add | solution.py:173
  143.5 1.5 collective-permute-start.6
  147.1 1.5 collective-permute-start.4
  149.5 1.7 fusion.292
  155.2 3.1 fusion.294
  158.4 2.1 fusion.295
  160.5 7.7 %bitcast_add_fusion.6 = (f32[512,1280]{0,1:T(8,128)}, f32[512,1280]{0,1:T(8,128)}) fusion(f32[20,512,64]{1,2,0:T(8,128)} %fusion.294, f32[512,1280]{0,1:T(8,128)} %get-tuple-element.528, pred[]{:T(512)S(6)} %compare.3, f32[20,512,64]{1,2,0:T(8,128)} %fusion.295, f32[512,1280]{0,1:T(8,128)} %get-tuple-element.527), kind=kLoop, calls=%fused_computation.11.clone.1 | loop fusion | flops 2621440 | bytes 15728641 | tf_op jit(solution)/shard_map/while/body/eval_jaxpr/add | solution.py:173
  168.8 2.2 multiply_convert_fusion
  172.6 7.7 %fusion.204 = f32[1280,2560]{1,0:T(8,128)} fusion(bf16[512,1280]{1,0:T(8,128)(2,1)S(1)} %copy-done.10, bf16[512,1280]{0,1:T(8,128)(2,1)S(1)} %convert.38, bf16[512,1280]{0,1:T(8,128)(2,1)S(1)} %multiply_convert_fusion), kind=kOutput, calls=%fused_computation.348 | convolution fusion | flops 3360686080 | bytes 17039360 | tf_op jit(solution)/shard_map/dot_general | solution.py:211
  180.6 7.0 %fusion.205 = f32[512,1280]{1,0:T(8,128)S(1)} fusion(bf16[1280,2560]{1,0:T(8,128)(2,1)} %all-gather.2.cloned.1.call-done, bf16[512,1280]{0,1:T(8,128)(2,1)} %copy-done.11, bf16[512,1280]{0,1:T(8,128)(2,1)S(1)} %multiply_convert_fusion), kind=kOutput, calls=%fused_computation.349 | convolution fusion | flops 3360686080 | bytes 11796480 | tf_op jit(solution)/shard_map/dot_general | solution.py:191
  187.7 6.7 %fusion.81 = (f32[1280]{0:T(1024)S(1)}, f32[1280]{0:T(1024)S(1)}, f32[1280]{0:T(1024)S(1)}, f32[1280]{0:T(1024)S(1)}, f32[1280]{0:T(1024)S(1)}, /*index=5*/f32[1...) fusion(bf16[1,527,1280]{2,1,0:T(8,128)(2,1)S(1)} %constant_dyna, ...), kind=kLoop, calls=%fused_computation.195 | loop fusion | flops 37335040 | bytes 27612160 | tf_op jit(solution)/shard_map/reduce_sum | solution.py:199
  194.6 2.6 fusion.52
  197.6 3.3 fusion.61
  202.3 4.6 collective-permute-start.11
  206.9 2.7 stack.127
  210.3 44.2 %psum.22 = f32[1280]{0:T(1024)} all-reduce(f32[1280]{0:T(1024)S(1)} %get-tuple-element.341), channel_id=1, replica_groups=mesh['dp'=16,'ctx'=2] {'dp','ctx'}, use_global_device_ids=true, to_apply=%region_39.40 | all-reduce | flops 1280 | bytes 10240 | tf_op jit(solution)/shard_map/psum | solution.py:209
  254.5 64.0 %reduce-scatter.2.cloned.1.call-done = f32[80,2560]{1,0:T(8,128)} async-done(((f32[1280,2560]{1,0:T(8,128)}), f32[80,2560]{1,0:T(8,128)}) %reduce-scatter.2.cloned.1.call-update) | async-done | bytes 819216 | tf_op jit(solution)/shard_map/reduce_scatter | solution.py:210
  318.8 43.9 %fusion.235 = bf16[1,512,1280]{2,1,0:T(8,128)(2,1)} fusion(f32[512,1280]{1,0:T(8,128)} %copy-done.6, f32[1,512,1280]{2,1,0:T(8,128)} %bitcast.634, f32[1,15,1280]{2,1,0:T(8,128)S(1)} %collective-permute-done.11, f32[1280]{0:T(1024)S(1)} %copy-done.33, f32[1280]{0:T(1024)S(1)} %copy-done.35, f32[1280]{0:T(1024)S(1)} %copy-done.39, f32[1280]{0:T(1024)S(1)} %copy-done.41, ...), kind=kLoop, calls=%fused_computation.396 | loop fusion | flops 60948480 | bytes 9487360 | tf_op jit(solution)/shard_map/broadcast_in_dim | solution.py:208
  362.7 83.9 %all-reduce.3.cloned.1.call-done = f32[31,1280]{1,0:T(8,128)} async-done(((f32[31,1280]{1,0:T(8,128)}), f32[31,1280]{1,0:T(8,128)}) %all-reduce.3.cloned.1.call-update) | async-done | bytes 158736 | tf_op jit(solution)/shard_map/psum | solution.py:209
  446.5 39.3 %all-reduce.5.cloned.1.call-done = f32[80,2560]{1,0:T(8,128)} async-done(((f32[80,2560]{1,0:T(8,128)}), f32[80,2560]{1,0:T(8,128)}) %all-reduce.5.cloned.1.call-update) | async-done | bytes 819216 | tf_op jit(solution)/shard_map/psum | solution.py:218
  485.9 1.6 copy.117
  487.5 2.1 copy.118
  (286 shorter events, 39.0 us)
Async XLA Ops:
  7.2 69.2 %all-gather.2.cloned.1.call-start = ((), (), s32[]{:S(2)}) async-start(), calls=%async_computation.1 | async-start | bytes 6963200 | tf_op jit(solution)/shard_map/all_gather | solution.py:114
  8.7 309.7 %reduce-scatter.2.cloned.1.call-start = ((), (), s32[]{:S(2)}) async-start(), calls=%async_computation.3 | async-start | bytes 13926400 | tf_op jit(solution)/shard_map/reduce_scatter | solution.py:210
  9.6 12.7 %collective-permute-start.8 = (bf16[1,15,1280]{2,1,0:T(8,128)(2,1)S(1)}, bf16[1,15,1280]{2,1,0:T(8,128)(2,1)S(1)}, u32[]{:S(2)}, u32[]{:S(2)}) collective-permute-start(bf16[1,15,1280]{2,1,0:T(8,128)(2,1)S(1)} %get-tuple-element.346), channel_id=1, source_target_pairs={{0,1},{2,3},{4,5},{6,7},{8,9},{10,11},{12,13},{14,15},{16,17},{18,... | collective-permute-start | bytes 115208 | tf_op jit(solution)/shard_map/ppermute | solution.py:14
  14.5 7.8 %collective-permute-start.9 = (bf16[1,15,1280]{2,1,0:T(8,128)(2,1)S(1)}, bf16[1,15,1280]{2,1,0:T(8,128)(2,1)S(1)}, u32[]{:S(2)}, u32[]{:S(2)}) collective-permute-start(bf16[1,15,1280]{2,1,0:T(8,128)(2,1)S(1)} %get-tuple-element.347), channel_id=1, source_target_pairs={{1,0},{3,2},{5,4},{7,6},{9,8},{11,10},{13,12},{15,14},{17,16},{19,... | collective-permute-start | bytes 115208 | tf_op jit(solution)/shard_map/ppermute | solution.py:17
  89.7 9.8 %collective-permute-start = (bf16[16,1280]{1,0:T(8,128)(2,1)S(1)}, bf16[16,1280]{1,0:T(8,128)(2,1)S(1)}, u32[]{:S(2)}, u32[]{:S(2)}) collective-permute-start(bf16[16,1280]{1,0:T(8,128)(2,1)S(1)} %copy.80), channel_id=1, source_target_pairs={{0,1},{1,0},{2,3},{3,2},{4,5},{5,4},{6,7},{7,6},{8,9},{9,8},{10,11... | collective-permute-start | bytes 122888 | tf_op jit(solution)/shard_map/while/body/eval_jaxpr/ppermute | solution.py:25
  94.3 5.1 %collective-permute-start.1 = (f32[16,1280]{1,0:T(8,128)S(1)}, f32[16,1280]{1,0:T(8,128)S(1)}, u32[]{:S(2)}, u32[]{:S(2)}) collective-permute-start(f32[16,1280]{1,0:T(8,128)S(1)} %add.1592), channel_id=1, source_target_pairs={{0,1},{1,0},{2,3},{3,2},{4,5},{5,4},{6,7},{7,6},{8,9},{9,8},{10,11... | collective-permute-start | bytes 245768 | tf_op jit(solution)/shard_map/while/body/eval_jaxpr/ppermute | solution.py:25
  95.7 3.8 collective-permute-start.2
  99.5 9.8 %collective-permute-start = (bf16[16,1280]{1,0:T(8,128)(2,1)S(1)}, bf16[16,1280]{1,0:T(8,128)(2,1)S(1)}, u32[]{:S(2)}, u32[]{:S(2)}) collective-permute-start(bf16[16,1280]{1,0:T(8,128)(2,1)S(1)} %copy.80), channel_id=1, source_target_pairs={{0,1},{1,0},{2,3},{3,2},{4,5},{5,4},{6,7},{7,6},{8,9},{9,8},{10,11... | collective-permute-start | bytes 122888 | tf_op jit(solution)/shard_map/while/body/eval_jaxpr/ppermute | solution.py:25
  104.1 5.1 %collective-permute-start.1 = (f32[16,1280]{1,0:T(8,128)S(1)}, f32[16,1280]{1,0:T(8,128)S(1)}, u32[]{:S(2)}, u32[]{:S(2)}) collective-permute-start(f32[16,1280]{1,0:T(8,128)S(1)} %add.1592), channel_id=1, source_target_pairs={{0,1},{1,0},{2,3},{3,2},{4,5},{5,4},{6,7},{7,6},{8,9},{9,8},{10,11... | collective-permute-start | bytes 245768 | tf_op jit(solution)/shard_map/while/body/eval_jaxpr/ppermute | solution.py:25
  105.5 3.8 collective-permute-start.2
  113.8 25.9 %collective-permute-start.5 = (f32[16,20]{0,1:T(8,128)}, f32[16,20]{0,1:T(8,128)}, u32[]{:S(2)}, u32[]{:S(2)}) collective-permute-start(f32[16,20]{0,1:T(8,128)} %copy.98), channel_id=1, source_target_pairs={{0,1},{1,0},{2,3},{3,2},{4,5},{5,4},{6,7},{7,6},{8,9},{9,8},{10,11... | collective-permute-start | bytes 3848 | tf_op jit(solution)/shard_map/while/body/eval_jaxpr/ppermute | solution.py:25
  116.6 23.1 %collective-permute-start.6 = (f32[16,20]{0,1:T(8,128)}, f32[16,20]{0,1:T(8,128)}, u32[]{:S(2)}, u32[]{:S(2)}) collective-permute-start(f32[16,20]{0,1:T(8,128)} %copy.99), channel_id=1, source_target_pairs={{0,1},{1,0},{2,3},{3,2},{4,5},{5,4},{6,7},{7,6},{8,9},{9,8},{10,11... | collective-permute-start | bytes 3848 | tf_op jit(solution)/shard_map/while/body/eval_jaxpr/ppermute | solution.py:25
  117.9 21.8 %collective-permute-start.3 = (bf16[16,1280]{1,0:T(8,128)(2,1)S(1)}, bf16[16,1280]{1,0:T(8,128)(2,1)}, u32[]{:S(2)}, u32[]{:S(2)}) collective-permute-start(bf16[16,1280]{1,0:T(8,128)(2,1)S(1)} %copy.96), channel_id=1, source_target_pairs={{0,1},{1,0},{2,3},{3,2},{4,5},{5,4},{6,7},{7,6},{8,9},{9,8},{10,11... | collective-permute-start | bytes 122888 | tf_op jit(solution)/shard_map/while/body/eval_jaxpr/ppermute | solution.py:25
  120.2 19.5 %collective-permute-start.4 = (bf16[16,1280]{1,0:T(8,128)(2,1)S(1)}, bf16[16,1280]{1,0:T(8,128)(2,1)}, u32[]{:S(2)}, u32[]{:S(2)}) collective-permute-start(bf16[16,1280]{1,0:T(8,128)(2,1)S(1)} %copy.97), channel_id=1, source_target_pairs={{0,1},{1,0},{2,3},{3,2},{4,5},{5,4},{6,7},{7,6},{8,9},{9,8},{10,11... | collective-permute-start | bytes 122888 | tf_op jit(solution)/shard_map/while/body/eval_jaxpr/ppermute | solution.py:25
  126.7 13.0 %collective-permute-start.7 = (f32[16,1280]{1,0:T(8,128)S(1)}, f32[16,1280]{1,0:T(8,128)S(1)}, u32[]{:S(2)}, u32[]{:S(2)}) collective-permute-start(f32[16,1280]{1,0:T(8,128)S(1)} %add.1597), channel_id=1, source_target_pairs={{0,1},{1,0},{2,3},{3,2},{4,5},{5,4},{6,7},{7,6},{8,9},{9,8},{10,11... | collective-permute-start | bytes 245768 | tf_op jit(solution)/shard_map/while/body/eval_jaxpr/ppermute | solution.py:25
  141.7 26.5 %collective-permute-start.5 = (f32[16,20]{0,1:T(8,128)}, f32[16,20]{0,1:T(8,128)}, u32[]{:S(2)}, u32[]{:S(2)}) collective-permute-start(f32[16,20]{0,1:T(8,128)} %copy.98), channel_id=1, source_target_pairs={{0,1},{1,0},{2,3},{3,2},{4,5},{5,4},{6,7},{7,6},{8,9},{9,8},{10,11... | collective-permute-start | bytes 3848 | tf_op jit(solution)/shard_map/while/body/eval_jaxpr/ppermute | solution.py:25
  143.5 24.6 %collective-permute-start.6 = (f32[16,20]{0,1:T(8,128)}, f32[16,20]{0,1:T(8,128)}, u32[]{:S(2)}, u32[]{:S(2)}) collective-permute-start(f32[16,20]{0,1:T(8,128)} %copy.99), channel_id=1, source_target_pairs={{0,1},{1,0},{2,3},{3,2},{4,5},{5,4},{6,7},{7,6},{8,9},{9,8},{10,11... | collective-permute-start | bytes 3848 | tf_op jit(solution)/shard_map/while/body/eval_jaxpr/ppermute | solution.py:25
  145.8 22.4 %collective-permute-start.3 = (bf16[16,1280]{1,0:T(8,128)(2,1)S(1)}, bf16[16,1280]{1,0:T(8,128)(2,1)}, u32[]{:S(2)}, u32[]{:S(2)}) collective-permute-start(bf16[16,1280]{1,0:T(8,128)(2,1)S(1)} %copy.96), channel_id=1, source_target_pairs={{0,1},{1,0},{2,3},{3,2},{4,5},{5,4},{6,7},{7,6},{8,9},{9,8},{10,11... | collective-permute-start | bytes 122888 | tf_op jit(solution)/shard_map/while/body/eval_jaxpr/ppermute | solution.py:25
  147.1 21.1 %collective-permute-start.4 = (bf16[16,1280]{1,0:T(8,128)(2,1)S(1)}, bf16[16,1280]{1,0:T(8,128)(2,1)}, u32[]{:S(2)}, u32[]{:S(2)}) collective-permute-start(bf16[16,1280]{1,0:T(8,128)(2,1)S(1)} %copy.97), channel_id=1, source_target_pairs={{0,1},{1,0},{2,3},{3,2},{4,5},{5,4},{6,7},{7,6},{8,9},{9,8},{10,11... | collective-permute-start | bytes 122888 | tf_op jit(solution)/shard_map/while/body/eval_jaxpr/ppermute | solution.py:25
  154.6 13.6 %collective-permute-start.7 = (f32[16,1280]{1,0:T(8,128)S(1)}, f32[16,1280]{1,0:T(8,128)S(1)}, u32[]{:S(2)}, u32[]{:S(2)}) collective-permute-start(f32[16,1280]{1,0:T(8,128)S(1)} %add.1597), channel_id=1, source_target_pairs={{0,1},{1,0},{2,3},{3,2},{4,5},{5,4},{6,7},{7,6},{8,9},{9,8},{10,11... | collective-permute-start | bytes 245768 | tf_op jit(solution)/shard_map/while/body/eval_jaxpr/ppermute | solution.py:25
  180.4 266.2 %all-reduce.3.cloned.1.call-start = ((), (), s32[]{:S(2)}) async-start(), calls=%async_computation.2 | async-start | bytes 327680 | tf_op jit(solution)/shard_map/psum | solution.py:209
  197.3 121.2 %copy-start.15 = (f32[1280]{0:T(1024)S(1)}, f32[1280]{0:T(1024)}, u32[]{:S(2)}) copy-start(f32[1280]{0:T(1024)} %copy-done.14) | copy-start | bytes 15364
  197.3 121.2 %copy-start.17 = (f32[1280]{0:T(1024)S(1)}, f32[1280]{0:T(1024)}, u32[]{:S(2)}) copy-start(f32[1280]{0:T(1024)} %copy-done.16) | copy-start | bytes 15364
  197.3 121.2 %copy-start.19 = (f32[1280]{0:T(1024)S(1)}, f32[1280]{0:T(1024)}, u32[]{:S(2)}) copy-start(f32[1280]{0:T(1024)} %copy-done.18) | copy-start | bytes 15364
  197.3 121.2 %copy-start.21 = (f32[1280]{0:T(1024)S(1)}, f32[1280]{0:T(1024)}, u32[]{:S(2)}) copy-start(f32[1280]{0:T(1024)} %copy-done.20) | copy-start | bytes 15364
  197.3 121.2 %copy-start.23 = (f32[1280]{0:T(1024)S(1)}, f32[1280]{0:T(1024)}, u32[]{:S(2)}) copy-start(f32[1280]{0:T(1024)} %copy-done.22) | copy-start | bytes 15364
  197.3 121.2 %copy-start.25 = (f32[1280]{0:T(1024)S(1)}, f32[1280]{0:T(1024)}, u32[]{:S(2)}) copy-start(f32[1280]{0:T(1024)} %copy-done.24) | copy-start | bytes 15364
  197.3 121.2 %copy-start.27 = (f32[1280]{0:T(1024)S(1)}, f32[1280]{0:T(1024)}, u32[]{:S(2)}) copy-start(f32[1280]{0:T(1024)} %copy-done.26) | copy-start | bytes 15364
  197.4 121.2 %copy-start.29 = (f32[1280]{0:T(1024)S(1)}, f32[1280]{0:T(1024)}, u32[]{:S(2)}) copy-start(f32[1280]{0:T(1024)} %copy-done.28) | copy-start | bytes 15364
  197.4 121.2 %copy-start.31 = (f32[1280]{0:T(1024)S(1)}, f32[1280]{0:T(1024)}, u32[]{:S(2)}) copy-start(f32[1280]{0:T(1024)} %copy-done.30) | copy-start | bytes 15364
  197.4 121.2 %copy-start.33 = (f32[1280]{0:T(1024)S(1)}, f32[1280]{0:T(1024)}, u32[]{:S(2)}) copy-start(f32[1280]{0:T(1024)} %copy-done.32) | copy-start | bytes 15364
  197.4 121.2 %copy-start.35 = (f32[1280]{0:T(1024)S(1)}, f32[1280]{0:T(1024)}, u32[]{:S(2)}) copy-start(f32[1280]{0:T(1024)} %copy-done.34) | copy-start | bytes 15364
  197.4 121.2 %copy-start.37 = (f32[1280]{0:T(1024)S(1)}, f32[1280]{0:T(1024)}, u32[]{:S(2)}) copy-start(f32[1280]{0:T(1024)} %copy-done.36) | copy-start | bytes 15364
  197.4 121.2 %copy-start.39 = (f32[1280]{0:T(1024)S(1)}, f32[1280]{0:T(1024)}, u32[]{:S(2)}) copy-start(f32[1280]{0:T(1024)} %copy-done.38) | copy-start | bytes 15364
  197.4 121.2 %copy-start.41 = (f32[1280]{0:T(1024)S(1)}, f32[1280]{0:T(1024)}, u32[]{:S(2)}) copy-start(f32[1280]{0:T(1024)} %copy-done.40) | copy-start | bytes 15364
  197.4 121.2 %copy-start.43 = (f32[1280]{0:T(1024)S(1)}, f32[1280]{0:T(1024)}, u32[]{:S(2)}) copy-start(f32[1280]{0:T(1024)} %copy-done.42) | copy-start | bytes 15364
  197.4 121.2 %copy-start.45 = (f32[1280]{0:T(1024)S(1)}, f32[1280]{0:T(1024)}, u32[]{:S(2)}) copy-start(f32[1280]{0:T(1024)} %copy-done.44) | copy-start | bytes 15364
  197.4 121.2 %copy-start.47 = (f32[1280]{0:T(1024)S(1)}, f32[1280]{0:T(1024)}, u32[]{:S(2)}) copy-start(f32[1280]{0:T(1024)} %copy-done.46) | copy-start | bytes 15364
  197.5 121.2 %copy-start.49 = (f32[1280]{0:T(1024)S(1)}, f32[1280]{0:T(1024)}, u32[]{:S(2)}) copy-start(f32[1280]{0:T(1024)} %copy-done.48) | copy-start | bytes 15364
  197.5 121.2 %copy-start.51 = (f32[1280]{0:T(1024)S(1)}, f32[1280]{0:T(1024)}, u32[]{:S(2)}) copy-start(f32[1280]{0:T(1024)} %copy-done.50) | copy-start | bytes 15364
  197.5 121.2 %copy-start.53 = (f32[1280]{0:T(1024)S(1)}, f32[1280]{0:T(1024)}, u32[]{:S(2)}) copy-start(f32[1280]{0:T(1024)} %copy-done.52) | copy-start | bytes 15364
  197.5 121.2 %copy-start.55 = (f32[1280]{0:T(1024)S(1)}, f32[1280]{0:T(1024)}, u32[]{:S(2)}) copy-start(f32[1280]{0:T(1024)} %copy-done.54) | copy-start | bytes 15364
  197.5 121.2 %copy-start.57 = (f32[1280]{0:T(1024)S(1)}, f32[1280]{0:T(1024)}, u32[]{:S(2)}) copy-start(f32[1280]{0:T(1024)} %copy-done.56) | copy-start | bytes 15364
  197.5 121.2 %copy-start.59 = (f32[1280]{0:T(1024)S(1)}, f32[1280]{0:T(1024)}, u32[]{:S(2)}) copy-start(f32[1280]{0:T(1024)} %copy-done.58) | copy-start | bytes 15364
  197.5 121.2 %copy-start.61 = (f32[1280]{0:T(1024)S(1)}, f32[1280]{0:T(1024)}, u32[]{:S(2)}) copy-start(f32[1280]{0:T(1024)} %copy-done.60) | copy-start | bytes 15364
  201.0 117.5 %collective-permute-start.10 = (f32[1,15,1280]{2,1,0:T(8,128)S(1)}, f32[1,15,1280]{2,1,0:T(8,128)S(1)}, u32[]{:S(2)}, u32[]{:S(2)}) collective-permute-start(f32[1,15,1280]{2,1,0:T(8,128)S(1)} %get-tuple-element.342), channel_id=1, source_target_pairs={{1,0},{3,2},{5,4},{7,6},{9,8},{11,10},{13,12},{15,14},{17,16},{19,... | collective-permute-start | bytes 230408 | tf_op jit(solution)/shard_map/ppermute | solution.py:17
  202.3 116.2 %collective-permute-start.11 = (f32[1,15,1280]{2,1,0:T(8,128)S(1)}, f32[1,15,1280]{2,1,0:T(8,128)S(1)}, u32[]{:S(2)}, u32[]{:S(2)}) collective-permute-start(f32[1,15,1280]{2,1,0:T(8,128)S(1)} %get-tuple-element.343), channel_id=1, source_target_pairs={{0,1},{2,3},{4,5},{6,7},{8,9},{10,11},{12,13},{14,15},{16,17},{18,... | collective-permute-start | bytes 230408 | tf_op jit(solution)/shard_map/ppermute | solution.py:14
  209.6 276.3 %all-reduce.5.cloned.1.call-start = ((), (), s32[]{:S(2)}) async-start(), calls=%async_computation.4 | async-start | bytes 1638400 | tf_op jit(solution)/shard_map/psum | solution.py:218
  (56 other events, 1331.7 us)
Sparse Core Ops, SparseCore 0:
  10.3 66.0 all-gather.1
  180.5 137.9 reduce-scatter.1
  325.5 120.9 all-reduce.2
  448.8 37.0 all-reduce.4
where the time goes:
time: 498 us; the launch traced here: 496 us
  waiting for transfers between devices  233 us (47%)
  other arithmetic  92.3 us (19%)
  blocking collectives  44.2 us (9%)
  matrix products  42.7 us (9%)
  local copies, waits for them, and re-layouts  37.5 us (8%)
  starting transfers between devices  29.8 us (6%)
  between operations  16 us (3%)
    psum x1, waiting for transfers between devices, per_device(): taps_grad, gain_grad = lax.psum((tap_terms, gain_term), ('dp', 'ctx'))  83.9 us
    reduce_scatter x1, waiting for transfers between devices, per_device(): lax.psum_scatter(lax.dot_general(encoded, kv_grad, (((0,), (0,)), ((), ()...  64 us
    psum x1, blocking collectives, per_device(): taps_grad, gain_grad = lax.psum((tap_terms, gain_term), ('dp', 'ctx'))  44.2 us
    broadcast_in_dim x1, other arithmetic, per_device(): frames_grad = (enc_grad + back_conv).astype(jnp.bfloat16)[None]  43.9 us
    all_gather x1, waiting for transfers between devices, per_device(): w_full = lax.all_gather(w_kv, 'dp', axis=0, tiled=True)  41.4 us
    psum x1, waiting for transfers between devices, per_device(): w_kv_grad = lax.psum(data_part, 'ctx')  39.3 us
    ppermute x16, starting transfers between devices, shifted(): return lax.ppermute(value, axis, pairs)  17.5 us
    unnamed x156, local copies, waits for them, and re-layouts  13.9 us
  transfers between devices with their start and end apart: 24, of which 6 were waited for; matrix products, arithmetic and copies ran while one was open for 27% of the time, Pallas kernels for 0%

commit v1 on v0

--- a/solution.py
+++ b/solution.py
@@ -206,7 +206,7 @@
         offset = 2 * rim_width - tap_idx
         back_conv = back_conv + conv_taps[tap_idx] * padded_grad[offset : offset + length]
     frames_grad = (enc_grad + back_conv).astype(jnp.bfloat16)[None]
-    taps_grad, gain_grad = lax.psum((tap_terms, gain_term), ("dp", "ctx"))
+    taps_grad, gain_grad = lax.psum(lax.psum((tap_terms, gain_term), "ctx"), "dp")
     data_part = lax.psum_scatter(
         lax.dot_general(
             encoded, kv_grad, (((0,), (0,)), ((), ())), preferred_element_type=jnp.float32

time: 498 us -> 461 us (0.926)
  waiting for transfers between devices: 233 us -> 204 us
  blocking collectives: 44.2 us -> 35.9 us
    psum x2, waiting for transfers between devices: 123 us -> 44.5 us  [the longest x1 44.5 us: per_device(): lax.psum(lax.psum((tap_terms, gain_term), 'ctx'), 'dp')]
    reduce_scatter x1, waiting for transfers between devices: 64 us -> 114 us  [per_device(): lax.psum_scatter(lax.dot_general(encoded, kv_grad, (((0,), (0,)), ((), ()...]
    psum x1 -> x2, blocking collectives: 44.2 us -> 35.9 us  [the longest x1 30.8 us: per_device(): lax.psum(lax.psum((tap_terms, gain_term), 'ctx'), 'dp')]
    unnamed x156 -> x158, local copies, waits for them, and re-layouts: 13.9 us -> 12.7 us
  transfers between devices with their start and end apart: 24 -> 24, of which waited for: 6 -> 5; matrix products, arithmetic and copies ran while one was open for 27% -> 29% of each run, Pallas kernels for 0% -> 0%
where the time goes in v1:
time: 461 us; the launch traced here: 459 us
  waiting for transfers between devices  204 us (44%)
  other arithmetic  92.3 us (20%)
  matrix products  42.7 us (9%)
  local copies, waits for them, and re-layouts  37.2 us (8%)
  blocking collectives  35.9 us (8%)
  starting transfers between devices  29.8 us (6%)
  between operations  16 us (3%)
    reduce_scatter x1, waiting for transfers between devices, per_device(): lax.psum_scatter(lax.dot_general(encoded, kv_grad, (((0,), (0,)), ((), ()...  114 us
    psum x1, waiting for transfers between devices, per_device(): lax.psum(lax.psum((tap_terms, gain_term), 'ctx'), 'dp')  44.5 us
    broadcast_in_dim x1, other arithmetic, per_device(): frames_grad = (enc_grad + back_conv).astype(jnp.bfloat16)[None]  43.9 us
    all_gather x1, waiting for transfers between devices, per_device(): w_full = lax.all_gather(w_kv, 'dp', axis=0, tiled=True)  41.4 us
    psum x1, blocking collectives, per_device(): lax.psum(lax.psum((tap_terms, gain_term), 'ctx'), 'dp')  30.8 us
    ppermute x16, starting transfers between devices, shifted(): return lax.ppermute(value, axis, pairs)  17.5 us
    add x2, other arithmetic, backward_turn(): value_acc + part_value  13.8 us
    unnamed x158, local copies, waits for them, and re-layouts  12.7 us
  transfers between devices with their start and end apart: 24, of which 5 were waited for; matrix products, arithmetic and copies ran while one was open for 29% of the time, Pallas kernels for 0%

profile of v1, /device:TPU:0, one launch (start us, length us, event | category | flops | bytes accessed | tf_op | source)
XLA Modules:
  0.0 458.6 jit_solution(4511399160331460453)
XLA Ops:
  7.2 1.5 copy.117
  9.6 4.8 %collective-permute-start.8 = (bf16[1,15,1280]{2,1,0:T(8,128)(2,1)S(1)}, bf16[1,15,1280]{2,1,0:T(8,128)(2,1)S(1)}, u32[]{:S(2)}, u32[]{:S(2)}) collective-permute-start(bf16[1,15,1280]{2,1,0:T(8,128)(2,1)S(1)} %get-tuple-element.348), channel_id=1, source_target_pairs={{0,1},{2,3},{4,5},{6,7},{8,9},{10,11},{12,13},{14,15},{16,17},{18,... | collective-permute-start | bytes 115208 | tf_op jit(solution)/shard_map/ppermute | solution.py:14
  16.4 1.5 slice_reduce_fusion.29
  18.0 1.8 slice_reduce_fusion.30
  19.9 1.5 constant_dynamic-update-slice_fusion.1
  22.3 12.4 %fusion.82 = (bf16[512,1280]{1,0:T(8,128)(2,1)}, f32[512,1280]{1,0:T(8,128)}) fusion(bf16[1,512,1280]{2,1,0:T(8,128)(2,1)S(1)} %copy-done.4, f32[1280]{0:T(1024)S(1)} %copy-done.76, bf16[1,527,1280]{2,1,0:T(8,128)(2,1)S(1)} %constant_dynamic-update-slice_fusion, f32[1280]{0:T(1024)S(1)} %get-tuple-element.290, f32[1280]{0:T(1024)S(1)} %get-tuple-element.291, ...), kind=kLoop, calls=%fused_computation.196 | loop fusion | flops 104202240 | bytes 25105920 | tf_op jit(solution)/shard_map/convert_element_type | solution.py:113
  35.0 41.4 %all-gather.2.cloned.1.call-done = bf16[1280,2560]{1,0:T(8,128)(2,1)} async-done(((bf16[80,2560]{1,0:T(8,128)(2,1)}), bf16[1280,2560]{1,0:T(8,128)(2,1)}) %all-gather.2.cloned.1.call-update) | async-done | bytes 6553616 | tf_op jit(solution)/shard_map/all_gather | solution.py:114
  76.4 6.8 %convolution_convert_fusion = bf16[512,2560]{1,0:T(8,128)(2,1)S(1)} fusion(bf16[512,1280]{1,0:T(8,128)(2,1)} %get-tuple-element.337, bf16[1280,2560]{1,0:T(8,128)(2,1)} %all-gather.2.cloned.1.call-done), kind=kOutput, calls=%fused_computation.72 | convolution fusion | flops 3356753920 | bytes 10485760 | tf_op jit(solution)/shard_map/dot_general | solution.py:115
  83.3 1.7 fusion.242
  85.0 1.6 copy.43
  86.6 2.4 copy.42
  89.6 19.6 %while.38 = (s32[]{:T(128)}, bf16[16,1280]{1,0:T(8,128)(2,1)S(1)}, f32[16,1280]{1,0:T(8,128)S(1)}, f32[16,20]{0,1:T(8,128)}, bf16[512,1280]{0,1:T(8,128)(2,1)}, ...) while((s32[]{:T(128)}, bf16[16,1280]{1,0:T(8,128)(2,1)S(1)}, ...), condition=%wide.region_2.3_spmd.clone, body=%wide.region_0.2_spmd.clone.sunk | while | flops 42620416 | bytes 4643037 | solution.py:153
  89.7 1.5 collective-permute-start
  92.0 1.7 fusion.280
  95.7 1.5 collective-permute-start.2
  97.1 2.3 collective-permute-done.2
  99.5 1.5 collective-permute-start
  101.8 1.7 fusion.280
  105.5 1.5 collective-permute-start.2
  106.9 2.3 collective-permute-done.2
  112.5 56.3 %while.39 = (s32[]{:T(128)}, bf16[16,1280]{1,0:T(8,128)(2,1)}, bf16[16,1280]{1,0:T(8,128)(2,1)}, f32[16,20]{0,1:T(8,128)}, f32[16,20]{0,1:T(8,128)}, /*index=5*/...) while((s32[]{:T(128)}, bf16[16,1280]{1,0:T(8,128)(2,1)}, ...), condition=%wide.region_5.6_spmd.clone, body=%wide.region_4.5_spmd.clone.sunk | while | flops 108647936 | bytes 37869488 | solution.py:185
  113.8 1.5 collective-permute-start.5
  117.9 1.5 collective-permute-start.3
  121.6 1.7 fusion.292
  126.7 1.5 collective-permute-start.7
  128.3 3.1 fusion.294
  131.4 2.1 fusion.295
  133.5 6.1 %bitcast_add_fusion.6 = (f32[512,1280]{0,1:T(8,128)}, f32[512,1280]{0,1:T(8,128)}) fusion(f32[20,512,64]{1,2,0:T(8,128)} %fusion.294, f32[512,1280]{0,1:T(8,128)} %get-tuple-element.530, pred[]{:T(512)S(6)} %compare.3, f32[20,512,64]{1,2,0:T(8,128)} %fusion.295, f32[512,1280]{0,1:T(8,128)} %get-tuple-element.529), kind=kLoop, calls=%fused_computation.11.clone.1 | loop fusion | flops 2621440 | bytes 15728641 | tf_op jit(solution)/shard_map/while/body/eval_jaxpr/add | solution.py:173
  143.5 1.5 collective-permute-start.6
  147.1 1.5 collective-permute-start.4
  149.5 1.7 fusion.292
  155.2 3.1 fusion.294
  158.4 2.1 fusion.295
  160.5 7.7 %bitcast_add_fusion.6 = (f32[512,1280]{0,1:T(8,128)}, f32[512,1280]{0,1:T(8,128)}) fusion(f32[20,512,64]{1,2,0:T(8,128)} %fusion.294, f32[512,1280]{0,1:T(8,128)} %get-tuple-element.530, pred[]{:T(512)S(6)} %compare.3, f32[20,512,64]{1,2,0:T(8,128)} %fusion.295, f32[512,1280]{0,1:T(8,128)} %get-tuple-element.529), kind=kLoop, calls=%fused_computation.11.clone.1 | loop fusion | flops 2621440 | bytes 15728641 | tf_op jit(solution)/shard_map/while/body/eval_jaxpr/add | solution.py:173
  168.8 2.2 multiply_convert_fusion
  172.6 7.7 %fusion.204 = f32[1280,2560]{1,0:T(8,128)} fusion(bf16[512,1280]{1,0:T(8,128)(2,1)S(1)} %copy-done.10, bf16[512,1280]{0,1:T(8,128)(2,1)S(1)} %convert.38, bf16[512,1280]{0,1:T(8,128)(2,1)S(1)} %multiply_convert_fusion), kind=kOutput, calls=%fused_computation.348 | convolution fusion | flops 3360686080 | bytes 17039360 | tf_op jit(solution)/shard_map/dot_general | solution.py:211
  180.6 7.0 %fusion.205 = f32[512,1280]{1,0:T(8,128)S(1)} fusion(bf16[1280,2560]{1,0:T(8,128)(2,1)} %all-gather.2.cloned.1.call-done, bf16[512,1280]{0,1:T(8,128)(2,1)} %copy-done.11, bf16[512,1280]{0,1:T(8,128)(2,1)S(1)} %multiply_convert_fusion), kind=kOutput, calls=%fused_computation.349 | convolution fusion | flops 3360686080 | bytes 11796480 | tf_op jit(solution)/shard_map/dot_general | solution.py:191
  187.7 6.7 %fusion.81 = (f32[1280]{0:T(1024)S(1)}, f32[1280]{0:T(1024)S(1)}, f32[1280]{0:T(1024)S(1)}, f32[1280]{0:T(1024)S(1)}, f32[1280]{0:T(1024)S(1)}, /*index=5*/f32[1...) fusion(bf16[1,527,1280]{2,1,0:T(8,128)(2,1)S(1)} %constant_dyna, ...), kind=kLoop, calls=%fused_computation.195 | loop fusion | flops 37335040 | bytes 27612160 | tf_op jit(solution)/shard_map/reduce_sum | solution.py:199
  194.6 2.6 fusion.52
  197.6 3.3 fusion.61
  201.0 2.7 stack.127
  203.7 113.8 %reduce-scatter.2.cloned.1.call-done = f32[80,2560]{1,0:T(8,128)} async-done(((f32[1280,2560]{1,0:T(8,128)}), f32[80,2560]{1,0:T(8,128)}) %reduce-scatter.2.cloned.1.call-update) | async-done | bytes 819216 | tf_op jit(solution)/shard_map/reduce_scatter | solution.py:210
  319.8 4.6 collective-permute-start.11
  325.0 5.1 %psum.37 = f32[1280]{0:T(1024)S(1)} all-reduce(f32[1280]{0:T(1024)S(1)} %get-tuple-element.343), channel_id=1, replica_groups=mesh['dp'=16,'ctx'=2] {'ctx'}, use_global_device_ids=true, to_apply=%region_40.41 | all-reduce | flops 1280 | bytes 10240 | tf_op jit(solution)/shard_map/psum | solution.py:209
  330.1 30.8 %psum.38 = f32[1280]{0:T(1024)} all-reduce(f32[1280]{0:T(1024)S(1)} %psum.37), channel_id=1, replica_groups=mesh['dp'=16,'ctx'=2] {'dp'}, use_global_device_ids=true, to_apply=%region_41.42 | all-reduce | flops 1280 | bytes 10240 | tf_op jit(solution)/shard_map/psum | solution.py:209
  361.2 43.9 %fusion.235 = bf16[1,512,1280]{2,1,0:T(8,128)(2,1)} fusion(f32[512,1280]{1,0:T(8,128)} %copy-done.6, f32[1,512,1280]{2,1,0:T(8,128)} %bitcast.634, f32[1,15,1280]{2,1,0:T(8,128)S(1)} %collective-permute-done.11, f32[1280]{0:T(1024)S(1)} %copy-done.34, f32[1280]{0:T(1024)S(1)} %copy-done.36, f32[1280]{0:T(1024)S(1)} %copy-done.40, f32[1280]{0:T(1024)S(1)} %copy-done.42, ...), kind=kLoop, calls=%fused_computation.396 | loop fusion | flops 60948480 | bytes 9487360 | tf_op jit(solution)/shard_map/broadcast_in_dim | solution.py:208
  405.1 44.5 %all-reduce.4.cloned.1.call-done = f32[31,1280]{1,0:T(8,128)} async-done(((f32[31,1280]{1,0:T(8,128)}), f32[31,1280]{1,0:T(8,128)}) %all-reduce.4.cloned.1.call-update) | async-done | bytes 158736 | tf_op jit(solution)/shard_map/psum | solution.py:209
  449.6 1.6 copy.118
  (289 shorter events, 39.3 us)
Async XLA Ops:
  7.2 69.2 %all-gather.2.cloned.1.call-start = ((), (), s32[]{:S(2)}) async-start(), calls=%async_computation.1 | async-start | bytes 6963200 | tf_op jit(solution)/shard_map/all_gather | solution.py:114
  8.7 308.7 %reduce-scatter.2.cloned.1.call-start = ((), (), s32[]{:S(2)}) async-start(), calls=%async_computation.3 | async-start | bytes 13926400 | tf_op jit(solution)/shard_map/reduce_scatter | solution.py:210
  9.6 12.7 %collective-permute-start.8 = (bf16[1,15,1280]{2,1,0:T(8,128)(2,1)S(1)}, bf16[1,15,1280]{2,1,0:T(8,128)(2,1)S(1)}, u32[]{:S(2)}, u32[]{:S(2)}) collective-permute-start(bf16[1,15,1280]{2,1,0:T(8,128)(2,1)S(1)} %get-tuple-element.348), channel_id=1, source_target_pairs={{0,1},{2,3},{4,5},{6,7},{8,9},{10,11},{12,13},{14,15},{16,17},{18,... | collective-permute-start | bytes 115208 | tf_op jit(solution)/shard_map/ppermute | solution.py:14
  14.5 7.8 %collective-permute-start.9 = (bf16[1,15,1280]{2,1,0:T(8,128)(2,1)S(1)}, bf16[1,15,1280]{2,1,0:T(8,128)(2,1)S(1)}, u32[]{:S(2)}, u32[]{:S(2)}) collective-permute-start(bf16[1,15,1280]{2,1,0:T(8,128)(2,1)S(1)} %get-tuple-element.349), channel_id=1, source_target_pairs={{1,0},{3,2},{5,4},{7,6},{9,8},{11,10},{13,12},{15,14},{17,16},{19,... | collective-permute-start | bytes 115208 | tf_op jit(solution)/shard_map/ppermute | solution.py:17
  89.7 9.8 %collective-permute-start = (bf16[16,1280]{1,0:T(8,128)(2,1)S(1)}, bf16[16,1280]{1,0:T(8,128)(2,1)S(1)}, u32[]{:S(2)}, u32[]{:S(2)}) collective-permute-start(bf16[16,1280]{1,0:T(8,128)(2,1)S(1)} %copy.80), channel_id=1, source_target_pairs={{0,1},{1,0},{2,3},{3,2},{4,5},{5,4},{6,7},{7,6},{8,9},{9,8},{10,11... | collective-permute-start | bytes 122888 | tf_op jit(solution)/shard_map/while/body/eval_jaxpr/ppermute | solution.py:25
  94.3 5.1 %collective-permute-start.1 = (f32[16,1280]{1,0:T(8,128)S(1)}, f32[16,1280]{1,0:T(8,128)S(1)}, u32[]{:S(2)}, u32[]{:S(2)}) collective-permute-start(f32[16,1280]{1,0:T(8,128)S(1)} %add.1596), channel_id=1, source_target_pairs={{0,1},{1,0},{2,3},{3,2},{4,5},{5,4},{6,7},{7,6},{8,9},{9,8},{10,11... | collective-permute-start | bytes 245768 | tf_op jit(solution)/shard_map/while/body/eval_jaxpr/ppermute | solution.py:25
  95.7 3.8 collective-permute-start.2
  99.5 9.8 %collective-permute-start = (bf16[16,1280]{1,0:T(8,128)(2,1)S(1)}, bf16[16,1280]{1,0:T(8,128)(2,1)S(1)}, u32[]{:S(2)}, u32[]{:S(2)}) collective-permute-start(bf16[16,1280]{1,0:T(8,128)(2,1)S(1)} %copy.80), channel_id=1, source_target_pairs={{0,1},{1,0},{2,3},{3,2},{4,5},{5,4},{6,7},{7,6},{8,9},{9,8},{10,11... | collective-permute-start | bytes 122888 | tf_op jit(solution)/shard_map/while/body/eval_jaxpr/ppermute | solution.py:25
  104.1 5.1 %collective-permute-start.1 = (f32[16,1280]{1,0:T(8,128)S(1)}, f32[16,1280]{1,0:T(8,128)S(1)}, u32[]{:S(2)}, u32[]{:S(2)}) collective-permute-start(f32[16,1280]{1,0:T(8,128)S(1)} %add.1596), channel_id=1, source_target_pairs={{0,1},{1,0},{2,3},{3,2},{4,5},{5,4},{6,7},{7,6},{8,9},{9,8},{10,11... | collective-permute-start | bytes 245768 | tf_op jit(solution)/shard_map/while/body/eval_jaxpr/ppermute | solution.py:25
  105.5 3.8 collective-permute-start.2
  113.8 25.9 %collective-permute-start.5 = (f32[16,20]{0,1:T(8,128)}, f32[16,20]{0,1:T(8,128)}, u32[]{:S(2)}, u32[]{:S(2)}) collective-permute-start(f32[16,20]{0,1:T(8,128)} %copy.98), channel_id=1, source_target_pairs={{0,1},{1,0},{2,3},{3,2},{4,5},{5,4},{6,7},{7,6},{8,9},{9,8},{10,11... | collective-permute-start | bytes 3848 | tf_op jit(solution)/shard_map/while/body/eval_jaxpr/ppermute | solution.py:25
  116.6 23.1 %collective-permute-start.6 = (f32[16,20]{0,1:T(8,128)}, f32[16,20]{0,1:T(8,128)}, u32[]{:S(2)}, u32[]{:S(2)}) collective-permute-start(f32[16,20]{0,1:T(8,128)} %copy.99), channel_id=1, source_target_pairs={{0,1},{1,0},{2,3},{3,2},{4,5},{5,4},{6,7},{7,6},{8,9},{9,8},{10,11... | collective-permute-start | bytes 3848 | tf_op jit(solution)/shard_map/while/body/eval_jaxpr/ppermute | solution.py:25
  117.9 21.8 %collective-permute-start.3 = (bf16[16,1280]{1,0:T(8,128)(2,1)S(1)}, bf16[16,1280]{1,0:T(8,128)(2,1)}, u32[]{:S(2)}, u32[]{:S(2)}) collective-permute-start(bf16[16,1280]{1,0:T(8,128)(2,1)S(1)} %copy.96), channel_id=1, source_target_pairs={{0,1},{1,0},{2,3},{3,2},{4,5},{5,4},{6,7},{7,6},{8,9},{9,8},{10,11... | collective-permute-start | bytes 122888 | tf_op jit(solution)/shard_map/while/body/eval_jaxpr/ppermute | solution.py:25
  120.2 19.5 %collective-permute-start.4 = (bf16[16,1280]{1,0:T(8,128)(2,1)S(1)}, bf16[16,1280]{1,0:T(8,128)(2,1)}, u32[]{:S(2)}, u32[]{:S(2)}) collective-permute-start(bf16[16,1280]{1,0:T(8,128)(2,1)S(1)} %copy.97), channel_id=1, source_target_pairs={{0,1},{1,0},{2,3},{3,2},{4,5},{5,4},{6,7},{7,6},{8,9},{9,8},{10,11... | collective-permute-start | bytes 122888 | tf_op jit(solution)/shard_map/while/body/eval_jaxpr/ppermute | solution.py:25
  126.7 13.0 %collective-permute-start.7 = (f32[16,1280]{1,0:T(8,128)S(1)}, f32[16,1280]{1,0:T(8,128)S(1)}, u32[]{:S(2)}, u32[]{:S(2)}) collective-permute-start(f32[16,1280]{1,0:T(8,128)S(1)} %add.1601), channel_id=1, source_target_pairs={{0,1},{1,0},{2,3},{3,2},{4,5},{5,4},{6,7},{7,6},{8,9},{9,8},{10,11... | collective-permute-start | bytes 245768 | tf_op jit(solution)/shard_map/while/body/eval_jaxpr/ppermute | solution.py:25
  141.7 26.5 %collective-permute-start.5 = (f32[16,20]{0,1:T(8,128)}, f32[16,20]{0,1:T(8,128)}, u32[]{:S(2)}, u32[]{:S(2)}) collective-permute-start(f32[16,20]{0,1:T(8,128)} %copy.98), channel_id=1, source_target_pairs={{0,1},{1,0},{2,3},{3,2},{4,5},{5,4},{6,7},{7,6},{8,9},{9,8},{10,11... | collective-permute-start | bytes 3848 | tf_op jit(solution)/shard_map/while/body/eval_jaxpr/ppermute | solution.py:25
  143.5 24.6 %collective-permute-start.6 = (f32[16,20]{0,1:T(8,128)}, f32[16,20]{0,1:T(8,128)}, u32[]{:S(2)}, u32[]{:S(2)}) collective-permute-start(f32[16,20]{0,1:T(8,128)} %copy.99), channel_id=1, source_target_pairs={{0,1},{1,0},{2,3},{3,2},{4,5},{5,4},{6,7},{7,6},{8,9},{9,8},{10,11... | collective-permute-start | bytes 3848 | tf_op jit(solution)/shard_map/while/body/eval_jaxpr/ppermute | solution.py:25
  145.8 22.4 %collective-permute-start.3 = (bf16[16,1280]{1,0:T(8,128)(2,1)S(1)}, bf16[16,1280]{1,0:T(8,128)(2,1)}, u32[]{:S(2)}, u32[]{:S(2)}) collective-permute-start(bf16[16,1280]{1,0:T(8,128)(2,1)S(1)} %copy.96), channel_id=1, source_target_pairs={{0,1},{1,0},{2,3},{3,2},{4,5},{5,4},{6,7},{7,6},{8,9},{9,8},{10,11... | collective-permute-start | bytes 122888 | tf_op jit(solution)/shard_map/while/body/eval_jaxpr/ppermute | solution.py:25
  147.1 21.1 %collective-permute-start.4 = (bf16[16,1280]{1,0:T(8,128)(2,1)S(1)}, bf16[16,1280]{1,0:T(8,128)(2,1)}, u32[]{:S(2)}, u32[]{:S(2)}) collective-permute-start(bf16[16,1280]{1,0:T(8,128)(2,1)S(1)} %copy.97), channel_id=1, source_target_pairs={{0,1},{1,0},{2,3},{3,2},{4,5},{5,4},{6,7},{7,6},{8,9},{9,8},{10,11... | collective-permute-start | bytes 122888 | tf_op jit(solution)/shard_map/while/body/eval_jaxpr/ppermute | solution.py:25
  154.6 13.6 %collective-permute-start.7 = (f32[16,1280]{1,0:T(8,128)S(1)}, f32[16,1280]{1,0:T(8,128)S(1)}, u32[]{:S(2)}, u32[]{:S(2)}) collective-permute-start(f32[16,1280]{1,0:T(8,128)S(1)} %add.1601), channel_id=1, source_target_pairs={{0,1},{1,0},{2,3},{3,2},{4,5},{5,4},{6,7},{7,6},{8,9},{9,8},{10,11... | collective-permute-start | bytes 245768 | tf_op jit(solution)/shard_map/while/body/eval_jaxpr/ppermute | solution.py:25
  180.4 180.5 %all-reduce.6.cloned.1.call-start = ((), (), s32[]{:S(2)}) async-start(), calls=%async_computation.4 | async-start | bytes 1966080 | tf_op jit(solution)/shard_map/psum | solution.py:209
  197.3 163.6 %copy-start.16 = (f32[1280]{0:T(1024)S(1)}, f32[1280]{0:T(1024)}, u32[]{:S(2)}) copy-start(f32[1280]{0:T(1024)} %copy-done.15) | copy-start | bytes 15364
  197.3 163.6 %copy-start.18 = (f32[1280]{0:T(1024)S(1)}, f32[1280]{0:T(1024)}, u32[]{:S(2)}) copy-start(f32[1280]{0:T(1024)} %copy-done.17) | copy-start | bytes 15364
  197.3 163.6 %copy-start.20 = (f32[1280]{0:T(1024)S(1)}, f32[1280]{0:T(1024)}, u32[]{:S(2)}) copy-start(f32[1280]{0:T(1024)} %copy-done.19) | copy-start | bytes 15364
  197.3 163.6 %copy-start.22 = (f32[1280]{0:T(1024)S(1)}, f32[1280]{0:T(1024)}, u32[]{:S(2)}) copy-start(f32[1280]{0:T(1024)} %copy-done.21) | copy-start | bytes 15364
  197.3 163.6 %copy-start.24 = (f32[1280]{0:T(1024)S(1)}, f32[1280]{0:T(1024)}, u32[]{:S(2)}) copy-start(f32[1280]{0:T(1024)} %copy-done.23) | copy-start | bytes 15364
  197.3 163.6 %copy-start.26 = (f32[1280]{0:T(1024)S(1)}, f32[1280]{0:T(1024)}, u32[]{:S(2)}) copy-start(f32[1280]{0:T(1024)} %copy-done.25) | copy-start | bytes 15364
  197.3 163.6 %copy-start.28 = (f32[1280]{0:T(1024)S(1)}, f32[1280]{0:T(1024)}, u32[]{:S(2)}) copy-start(f32[1280]{0:T(1024)} %copy-done.27) | copy-start | bytes 15364
  197.3 163.6 %copy-start.30 = (f32[1280]{0:T(1024)S(1)}, f32[1280]{0:T(1024)}, u32[]{:S(2)}) copy-start(f32[1280]{0:T(1024)} %copy-done.29) | copy-start | bytes 15364
  197.4 163.6 %copy-start.32 = (f32[1280]{0:T(1024)S(1)}, f32[1280]{0:T(1024)}, u32[]{:S(2)}) copy-start(f32[1280]{0:T(1024)} %copy-done.31) | copy-start | bytes 15364
  197.4 163.6 %copy-start.34 = (f32[1280]{0:T(1024)S(1)}, f32[1280]{0:T(1024)}, u32[]{:S(2)}) copy-start(f32[1280]{0:T(1024)} %copy-done.33) | copy-start | bytes 15364
  197.4 163.6 %copy-start.36 = (f32[1280]{0:T(1024)S(1)}, f32[1280]{0:T(1024)}, u32[]{:S(2)}) copy-start(f32[1280]{0:T(1024)} %copy-done.35) | copy-start | bytes 15364
  197.4 163.6 %copy-start.38 = (f32[1280]{0:T(1024)S(1)}, f32[1280]{0:T(1024)}, u32[]{:S(2)}) copy-start(f32[1280]{0:T(1024)} %copy-done.37) | copy-start | bytes 15364
  197.4 163.6 %copy-start.40 = (f32[1280]{0:T(1024)S(1)}, f32[1280]{0:T(1024)}, u32[]{:S(2)}) copy-start(f32[1280]{0:T(1024)} %copy-done.39) | copy-start | bytes 15364
  197.4 163.6 %copy-start.42 = (f32[1280]{0:T(1024)S(1)}, f32[1280]{0:T(1024)}, u32[]{:S(2)}) copy-start(f32[1280]{0:T(1024)} %copy-done.41) | copy-start | bytes 15364
  197.4 163.6 %copy-start.44 = (f32[1280]{0:T(1024)S(1)}, f32[1280]{0:T(1024)}, u32[]{:S(2)}) copy-start(f32[1280]{0:T(1024)} %copy-done.43) | copy-start | bytes 15364
  197.4 163.6 %copy-start.46 = (f32[1280]{0:T(1024)S(1)}, f32[1280]{0:T(1024)}, u32[]{:S(2)}) copy-start(f32[1280]{0:T(1024)} %copy-done.45) | copy-start | bytes 15364
  197.4 163.6 %copy-start.48 = (f32[1280]{0:T(1024)S(1)}, f32[1280]{0:T(1024)}, u32[]{:S(2)}) copy-start(f32[1280]{0:T(1024)} %copy-done.47) | copy-start | bytes 15364
  197.4 163.6 %copy-start.50 = (f32[1280]{0:T(1024)S(1)}, f32[1280]{0:T(1024)}, u32[]{:S(2)}) copy-start(f32[1280]{0:T(1024)} %copy-done.49) | copy-start | bytes 15364
  197.5 163.6 %copy-start.52 = (f32[1280]{0:T(1024)S(1)}, f32[1280]{0:T(1024)}, u32[]{:S(2)}) copy-start(f32[1280]{0:T(1024)} %copy-done.51) | copy-start | bytes 15364
  197.5 163.6 %copy-start.54 = (f32[1280]{0:T(1024)S(1)}, f32[1280]{0:T(1024)}, u32[]{:S(2)}) copy-start(f32[1280]{0:T(1024)} %copy-done.53) | copy-start | bytes 15364
  197.5 163.6 %copy-start.56 = (f32[1280]{0:T(1024)S(1)}, f32[1280]{0:T(1024)}, u32[]{:S(2)}) copy-start(f32[1280]{0:T(1024)} %copy-done.55) | copy-start | bytes 15364
  197.5 163.6 %copy-start.58 = (f32[1280]{0:T(1024)S(1)}, f32[1280]{0:T(1024)}, u32[]{:S(2)}) copy-start(f32[1280]{0:T(1024)} %copy-done.57) | copy-start | bytes 15364
  197.5 163.6 %copy-start.60 = (f32[1280]{0:T(1024)S(1)}, f32[1280]{0:T(1024)}, u32[]{:S(2)}) copy-start(f32[1280]{0:T(1024)} %copy-done.59) | copy-start | bytes 15364
  197.5 163.6 %copy-start.62 = (f32[1280]{0:T(1024)S(1)}, f32[1280]{0:T(1024)}, u32[]{:S(2)}) copy-start(f32[1280]{0:T(1024)} %copy-done.61) | copy-start | bytes 15364
  317.5 132.1 %all-reduce.4.cloned.1.call-start = ((), (), s32[]{:S(2)}) async-start(), calls=%async_computation.2 | async-start | bytes 327680 | tf_op jit(solution)/shard_map/psum | solution.py:209
  318.5 42.4 %collective-permute-start.10 = (f32[1,15,1280]{2,1,0:T(8,128)S(1)}, f32[1,15,1280]{2,1,0:T(8,128)S(1)}, u32[]{:S(2)}, u32[]{:S(2)}) collective-permute-start(f32[1,15,1280]{2,1,0:T(8,128)S(1)} %get-tuple-element.344), channel_id=1, source_target_pairs={{1,0},{3,2},{5,4},{7,6},{9,8},{11,10},{13,12},{15,14},{17,16},{19,... | collective-permute-start | bytes 230408 | tf_op jit(solution)/shard_map/ppermute | solution.py:17
  319.8 41.1 %collective-permute-start.11 = (f32[1,15,1280]{2,1,0:T(8,128)S(1)}, f32[1,15,1280]{2,1,0:T(8,128)S(1)}, u32[]{:S(2)}, u32[]{:S(2)}) collective-permute-start(f32[1,15,1280]{2,1,0:T(8,128)S(1)} %get-tuple-element.345), channel_id=1, source_target_pairs={{0,1},{2,3},{4,5},{6,7},{8,9},{10,11},{12,13},{14,15},{16,17},{18,... | collective-permute-start | bytes 230408 | tf_op jit(solution)/shard_map/ppermute | solution.py:14
  (57 other events, 1790.8 us)
Sparse Core Ops, SparseCore 0:
  10.3 66.0 all-gather.1
  180.5 136.9 reduce-scatter.1
  320.5 37.9 all-reduce.5
  361.8 87.7 all-reduce.3
